TPU v7x, 32 devices: a whole 2x2x4 slice. The times are simulated.
32 devices in a mesh: space: 4 (over x, core), energy: 8 (over z, y).
Axes of the slice: x: 2, y: 2, z: 4, core: 2. Of those that a mesh axis runs over, the one named last changes fastest.
Arguments:
- green_lower: bfloat16 [4, 32, 2, 128, 128], P('space', 'energy'), may hold values from -0.5 to 0.5
- green_diag: bfloat16 [4, 32, 2, 128, 128], P('space', 'energy'), may hold values from -0.5 to 0.5
- green_upper: bfloat16 [4, 32, 2, 128, 128], P('space', 'energy'), may hold values from -0.5 to 0.5
- self_energy: bfloat16 [2, 4, 32, 2, 128, 128], P(None, 'space', 'energy'), may hold values from -1.75 to 1.75
- coulomb: bfloat16 [4, 128, 128], P('space'), may hold values from -0.5 to 0.5
Outputs:
- screened_polarization: bfloat16 [2, 4, 32, 2, 128, 128], P(None, 'space', 'energy')
All inputs are finite; a program needn't handle non-finite values.
Results may differ from a plain program's by a relative error of at most 0.017.
Values may be sent and summed in bfloat16 or wider, within the bound.
A program may use at most 64 MiB of HBM per device.

v0:
```python
import functools
import math

import jax
import jax.numpy as jnp
from jax import lax
from jax.experimental import pallas as pl
from jax.experimental.pallas import tpu as pltpu
from jax.sharding import PartitionSpec as P


def padded_2(shard, sides, width):
    for axis, dim in sides:
        peers, length = (lax.axis_size(axis), shard.shape[dim])
        up = [(i, (i + 1) % peers) for i in range(peers - 1)]
        down = [(j, i) for i, j in up]
        last = lax.slice_in_dim(shard, length - width, length, axis=dim)
        initial = lax.slice_in_dim(shard, 0, width, axis=dim)
        before = lax.ppermute(last, axis, up)
        after = lax.ppermute(initial, axis, down)
        shard = jnp.concatenate([before, shard, after], axis=dim)
    return shard


def congruence(green, sigma):
    green_real = green[:, :, 0]
    green_imag = green[:, :, 1]
    sigma_real = sigma[:, :, :, 0]
    sigma_imag = sigma[:, :, :, 1]
    green_wide = jnp.concatenate([green_real, green_imag], axis=-1)
    sigma_tall = jnp.concatenate(
        [
            jnp.concatenate([sigma_real, sigma_imag], axis=-1),
            jnp.concatenate([-sigma_imag, sigma_real], axis=-1),
        ],
        axis=-2,
    )
    mixed = jnp.einsum(
        "nepq,fneqr->fnepr", green_wide, sigma_tall, preferred_element_type=jnp.float32
    ).astype(jnp.bfloat16)
    adjoint_tall = jnp.concatenate(
        [green_wide, jnp.concatenate([-green_imag, green_real], axis=-1)], axis=-2
    )
    return jnp.einsum("fnepr,nesr->fneps", mixed, adjoint_tall, preferred_element_type=jnp.float32)


def split_table(table):
    high_part = table.astype(jnp.bfloat16)
    low_part = (table - high_part.astype(jnp.float32)).astype(jnp.bfloat16)
    return (high_part, low_part)


def spectrum(values, table_high, table_low, padded_len):

    def apply_table(part):
        return jnp.dot(table_high, part, preferred_element_type=jnp.float32) + jnp.dot(
            table_low, part, preferred_element_type=jnp.float32
        )

    real_terms = apply_table(values[:, 0])
    imag_terms = apply_table(values[:, 1])
    out_real = real_terms[:padded_len] + imag_terms[padded_len:]
    out_imag = imag_terms[:padded_len] - real_terms[padded_len:]
    return (out_real, out_imag)


def plain_body(green_lower, green_diag, green_upper, self_energy, coulomb):
    block_count = green_diag.shape[0]
    energy_local = green_diag.shape[1]
    block_order = green_diag.shape[-1]
    energies = energy_local * lax.axis_size("energy")
    padded_len = 2 * energies
    padded = padded_2(self_energy, (("space", 1),), 1)
    lower_term = congruence(green_lower, padded[:, :block_count])
    diag_term = congruence(green_diag, padded[:, 1 : block_count + 1])
    upper_term = congruence(green_upper, padded[:, 2:])
    total = lower_term + diag_term + upper_term
    total = total.reshape(2, block_count, energy_local, block_order, 2, block_order)
    green_function = (
        jnp.transpose(total, (0, 2, 4, 1, 3, 5))
        .astype(jnp.bfloat16)
        .reshape(2, energy_local, 2, -1)
    )
    frequency = lax.iota(jnp.int32, padded_len)
    energy_index = lax.iota(jnp.int32, energies)
    step_angle = 2.0 * math.pi / padded_len
    forward_angle = (frequency[:, None] * energy_index[None, :] % padded_len).astype(
        jnp.float32
    ) * step_angle
    forward_table = jnp.concatenate([jnp.cos(forward_angle), jnp.sin(forward_angle)], axis=0)
    table_high, table_low = split_table(forward_table)
    lesser_values = lax.all_to_all(
        green_function[0], "energy", split_axis=2, concat_axis=0, tiled=True
    )
    greater_values = lax.all_to_all(
        green_function[1], "energy", split_axis=2, concat_axis=0, tiled=True
    )
    lesser_real, lesser_imag = spectrum(lesser_values, table_high, table_low, padded_len)
    greater_real, greater_imag = spectrum(greater_values, table_high, table_low, padded_len)
    product_real = lesser_real * greater_real + lesser_imag * greater_imag
    product_imag = lesser_imag * greater_real - lesser_real * greater_imag
    row_index = jnp.concatenate([energy_index, (padded_len - energy_index) % padded_len])
    back_angle = (row_index[:, None] * frequency[None, :] % padded_len).astype(
        jnp.float32
    ) * step_angle
    back_cos = jnp.cos(back_angle)
    back_sin = jnp.sin(back_angle)
    back_table = jnp.concatenate(
        [
            jnp.concatenate([back_cos, -back_sin], axis=1),
            jnp.concatenate([back_sin, back_cos], axis=1),
        ],
        axis=0,
    )
    stacked_product = jnp.concatenate([product_real, product_imag], axis=0)
    factor = 1.0 / (padded_len * math.sqrt(energies))
    combined = (
        jnp.dot(
            back_table,
            stacked_product,
            precision=lax.Precision.HIGH,
            preferred_element_type=jnp.float32,
        )
        * factor
    )
    corr_real = combined[:padded_len]
    corr_imag = combined[padded_len:]
    lesser_lags = jnp.stack([corr_real[:energies], corr_imag[:energies]], axis=1)
    greater_lags = jnp.stack([corr_real[energies:], -corr_imag[energies:]], axis=1)
    polar = jnp.stack([lesser_lags, greater_lags], axis=0).astype(jnp.bfloat16)
    returned = lax.all_to_all(polar, "energy", split_axis=1, concat_axis=3, tiled=True)
    returned = returned.reshape(2, energy_local, 2, block_count, block_order, block_order)
    left_product = jnp.einsum(
        "npq,fetnqr->fetnpr", coulomb, returned, preferred_element_type=jnp.float32
    ).astype(jnp.bfloat16)
    screened = jnp.einsum(
        "fetnpr,nsr->fnetps", left_product, coulomb, preferred_element_type=jnp.float32
    )
    return screened.astype(jnp.bfloat16)


ROWS = 16
MESH = pl.DeviceIdType.MESH


def partner(me, step):
    other, bit = me, 1
    while bit <= step:
        if step & bit:
            other = other + bit * (1 - 2 * lax.rem(lax.div(me, bit), 2))
        bit *= 2
    return other


def alternate(peers):
    far, near = list(range(peers // 2, peers)), list(range(1, peers // 2))
    steps = []
    for i in range(peers // 2):
        steps += far[i : i + 1] + near[i : i + 1]
    return steps


def rotation(real, imag):
    return jnp.concatenate(
        [
            jnp.concatenate([real, imag], axis=1),
            jnp.concatenate([-imag, real], axis=1),
        ],
        axis=0,
    )


def fused_kernel(
    peers,
    sites,
    lower_hbm,
    diag_hbm,
    upper_hbm,
    sigma_hbm,
    coulomb_hbm,
    out_hbm,
    greens,
    sigma_ref,
    coulomb_ref,
    halo,
    total,
    green_out,
    green_in,
    series,
    polar_out,
    polar_in,
    out_ref,
    out_sem,
    load_sem,
    coulomb_sem,
    halo_send,
    halo_recv,
    green_send,
    green_recv,
    polar_send,
    polar_recv,
):
    me = lax.axis_index("energy")
    site = lax.axis_index("space")
    has_next = site < sites - 1
    has_previous = site > 0
    next_site = lax.rem(site + 1, sites)
    previous_site = lax.rem(site + sites - 1, sites)
    local, order = greens.shape[0], greens.shape[-1]
    half = order // 2
    energies = peers * local
    steps = alternate(peers)
    f32, bf16 = jnp.float32, jnp.bfloat16

    barrier = pltpu.get_barrier_semaphore()
    for step in steps:
        pl.semaphore_signal(
            barrier, inc=1, device_id={"energy": partner(me, step)}, device_id_type=MESH
        )

    @pl.when(has_next)
    def _():
        pl.semaphore_signal(barrier, inc=1, device_id={"space": next_site}, device_id_type=MESH)

    @pl.when(has_previous)
    def _():
        pl.semaphore_signal(barrier, inc=1, device_id={"space": previous_site}, device_id_type=MESH)

    def load_sigma(energy):
        return pltpu.make_async_copy(
            sigma_hbm.at[:, 0, energy], sigma_ref.at[:, energy], load_sem.at[energy, 0]
        )

    sources = (diag_hbm, lower_hbm, upper_hbm)
    for energy in range(local):
        load_sigma(energy).start()
        for i, source in enumerate(sources):
            pltpu.make_async_copy(
                source.at[0, energy], greens.at[energy, i], load_sem.at[energy, 1]
            ).start()
    coulomb_load = pltpu.make_async_copy(coulomb_hbm.at[0], coulomb_ref, coulomb_sem)
    coulomb_load.start()

    neighbours = jnp.where(has_next, 1, 0) + jnp.where(has_previous, 1, 0)
    pl.semaphore_wait(barrier, peers - 1 + neighbours)

    def halo_copy(side, energy):
        return pltpu.make_async_remote_copy(
            src_ref=sigma_hbm.at[:, 0, energy],
            dst_ref=halo.at[side, energy],
            send_sem=halo_send.at[side, energy],
            recv_sem=halo_recv.at[side, energy],
            device_id={"space": next_site if side == 0 else previous_site},
            device_id_type=MESH,
        )

    def each_halo(energy, act):
        @pl.when(has_next)
        def _():
            act(halo_copy(0, energy))

        @pl.when(has_previous)
        def _():
            act(halo_copy(1, energy))

    for energy in range(min(2, local)):
        each_halo(energy, lambda copy: copy.start())

    @pl.when(jnp.logical_not(has_previous))
    def _():
        halo[0] = jnp.zeros(halo.shape[1:], halo.dtype)

    @pl.when(jnp.logical_not(has_next))
    def _():
        halo[1] = jnp.zeros(halo.shape[1:], halo.dtype)

    def green_copy(side, other, slot, first, count):
        return pltpu.make_async_remote_copy(
            src_ref=green_out.at[side, other, pl.ds(first, count)],
            dst_ref=green_in.at[side, slot, pl.ds(first, count)],
            send_sem=green_send,
            recv_sem=green_recv.at[side, slot],
            device_id={"energy": other},
            device_id_type=MESH,
        )

    def send_green(side, first, count):
        for step in steps:
            green_copy(side, partner(me, step), me, first, count).start()

    def term(energy, terms):
        mixed, adjoint = [], []
        for which, sigma_of in terms:
            real, imag = greens[energy, which, 0], greens[energy, which, 1]
            wide = jnp.concatenate([real, imag], axis=1)
            mixed.append(
                jnp.concatenate(
                    [
                        jnp.dot(
                            wide,
                            rotation(sigma_of(kind, 0), sigma_of(kind, 1)),
                            preferred_element_type=f32,
                        ).astype(bf16)
                        for kind in range(2)
                    ],
                    axis=0,
                )
            )
            adjoint.append(
                jnp.concatenate(
                    [rotation(real[:half], imag[:half]), rotation(real[half:], imag[half:])],
                    axis=0,
                )
            )
        return lax.dot_general(
            jnp.concatenate(mixed, axis=1),
            jnp.concatenate(adjoint, axis=1),
            (((1,), (1,)), ((), ())),
            preferred_element_type=f32,
        )

    def own_term(energy):
        load_sigma(energy).wait()
        pltpu.make_async_copy(greens.at[energy], greens.at[energy], load_sem.at[energy, 1]).wait()
        total[energy] = term(energy, [(0, lambda kind, part: sigma_ref[kind, energy, part])])

    for energy in range(min(2, local)):
        own_term(energy)
    for energy in range(local):

        @pl.when(has_previous)
        def _():
            halo_copy(0, energy).wait_recv()

        @pl.when(has_next)
        def _():
            halo_copy(1, energy).wait_recv()

        each_halo(energy, lambda copy: copy.wait_send())
        if energy + 2 < local:
            each_halo(energy + 2, lambda copy: copy.start())
        coupled = term(
            energy,
            [
                (1, lambda kind, part: halo[0, energy, kind, part]),
                (2, lambda kind, part: halo[1, energy, kind, part]),
            ],
        )
        rounded = (total[energy] + coupled).astype(bf16)
        for side in range(2):
            for kind in range(2):
                block = rounded[
                    kind * order : (kind + 1) * order, side * order : (side + 1) * order
                ]
                green_out[side, :, energy, kind] = block.reshape(peers, ROWS, order)
        first = energy - energy % 2
        if energy % 2 == 1 or energy == local - 1:
            for side in range(2):
                send_green(side, first, energy + 1 - first)
        if energy + 2 < local:
            own_term(energy + 2)

    coulomb_load.wait()
    coulomb = coulomb_ref[...]
    in_low = lax.broadcasted_iota(jnp.int32, (order, order), 1) < half
    straight = coulomb.astype(f32)
    swapped = pltpu.roll(straight, half, 1)
    zeros = jnp.zeros_like(straight)
    spread = jnp.concatenate(
        [
            jnp.concatenate(
                [jnp.where(in_low, straight, zeros), jnp.where(in_low, swapped, zeros)], axis=1
            ),
            jnp.concatenate(
                [jnp.where(in_low, zeros, swapped), jnp.where(in_low, zeros, straight)], axis=1
            ),
        ],
        axis=0,
    ).astype(bf16)

    fold = ROWS // 2
    low_lanes = lax.broadcasted_iota(jnp.int32, (local, fold, order), 2) < half

    def swap(values):
        return pltpu.roll(values.reshape(-1, order), half, 1).reshape(values.shape)

    tail = series.shape[3] - energies
    for side in range(2):
        for kind in range(2):
            for part in range(2):
                series[side, kind, part, energies:] = jnp.zeros((tail, fold, order), f32)

    def unpack(side, source, values):
        for kind in range(2):
            tile = values[:, kind].astype(f32)
            top, bottom = tile[:, :fold], tile[:, fold:]
            where = pl.ds(source * local, local)
            series[side, kind, 0, where] = jnp.where(low_lanes, top, swap(bottom))
            series[side, kind, 1, where] = jnp.where(low_lanes, swap(top), bottom)

    def receive_green(side):
        unpack(side, me, green_out[side, me])
        for step in steps:
            other = partner(me, step)
            green_copy(side, other, other, 0, local).wait_recv()
            unpack(side, other, green_in[side, other])

    factor = 1.0 / math.sqrt(energies)

    def correlate(side, owner):
        first_lag = owner * local

        def some_energies(index, sums):
            start = index * local
            window = pl.ds(start + first_lag, 2 * local - 1)
            results = []
            for kind in range(2):
                sum_real, sum_imag = sums[2 * kind : 2 * kind + 2]
                ahead_real, ahead_imag = series[side, kind, 0, window], series[side, kind, 1, window]
                for i in range(local):
                    real = series[side, 1 - kind, 0, start + i]
                    imag = series[side, 1 - kind, 1, start + i]
                    shifted_real, shifted_imag = ahead_real[i : i + local], ahead_imag[i : i + local]
                    sum_real = sum_real + (shifted_real * real + shifted_imag * imag)
                    sum_imag = sum_imag + (shifted_imag * real - shifted_real * imag)
                results += [sum_real, sum_imag]
            return tuple(results)

        zero = jnp.zeros((local, fold, order), f32)
        sums = lax.fori_loop(0, peers - owner, some_energies, (zero,) * 4)
        tiles = []
        for kind in range(2):
            real, imag = sums[2 * kind] * factor, sums[2 * kind + 1] * factor
            top = jnp.where(low_lanes, real, swap(imag))
            bottom = jnp.where(low_lanes, swap(real), imag)
            tiles.append(jnp.concatenate([top, bottom], axis=1).astype(bf16))
        return tiles

    def polar_copy(side, other, slot, kind):
        return pltpu.make_async_remote_copy(
            src_ref=polar_out.at[side, kind, other],
            dst_ref=polar_in.at[side, kind, slot],
            send_sem=polar_send,
            recv_sem=polar_recv.at[side, kind],
            device_id={"energy": other},
            device_id_type=MESH,
        )

    for side in range(2):
        receive_green(side)
        for step in steps:
            other = partner(me, step)
            tiles = correlate(side, other)
            for kind in range(2):
                polar_out[side, kind, other] = tiles[kind]
            for kind in range(2 if side == 0 else 1):
                polar_copy(side, other, me, kind).start()
        if side == 1:
            for step in steps:
                polar_copy(side, partner(me, step), me, 1).start()
        tiles = correlate(side, me)
        for kind in range(2):
            polar_in[side, kind, me] = tiles[kind]

    def out_copy(kind):
        return pltpu.make_async_copy(out_ref.at[kind], out_hbm.at[kind, 0], out_sem.at[kind])

    for kind in range(2):
        for side in range(2):
            arrived = polar_in.at[side, kind, pl.ds(0, peers - 1)]
            pltpu.make_async_copy(arrived, arrived, polar_recv.at[side, kind]).wait()
        lefts = []
        for lag in range(local):
            both = jnp.concatenate(
                [polar_in[side, kind, :, lag].reshape(order, order) for side in range(2)], axis=1
            )
            lefts.append(jnp.dot(coulomb, both, preferred_element_type=f32).astype(bf16))
        screened = lax.dot_general(
            jnp.concatenate(lefts, axis=0),
            spread,
            (((1,), (1,)), ((), ())),
            preferred_element_type=f32,
        ).astype(bf16)
        for lag in range(local):
            rows = screened[lag * order : (lag + 1) * order]
            out_ref[kind, lag, 0] = rows[:, :order]
            out_ref[kind, lag, 1] = rows[:, order:]
        out_copy(kind).start()

    for sent, sem in ((green_out, green_send), (polar_out, polar_send)):
        if sent is green_out:
            part = sent.at[:, pl.ds(0, peers - 1)]
        else:
            part = sent.at[:, :, pl.ds(0, peers - 1)]
        pltpu.make_async_copy(part, part, sem).wait()
    for kind in range(2):
        out_copy(kind).wait()


def fused_body(green_lower, green_diag, green_upper, self_energy, coulomb):
    peers, sites = lax.axis_size("energy"), lax.axis_size("space")
    local, order = green_diag.shape[1], green_diag.shape[-1]
    bf16 = jnp.bfloat16
    share = (2, peers, local, 2, ROWS, order)
    lags = (2, 2, peers, local, ROWS, order)
    series = (2, 2, 2, peers * local + local, ROWS // 2, order)
    dma = pltpu.SemaphoreType.DMA
    return pl.pallas_call(
        functools.partial(fused_kernel, peers, sites),
        out_shape=jax.ShapeDtypeStruct(self_energy.shape, bf16),
        in_specs=[pl.BlockSpec(memory_space=pltpu.HBM)] * 5,
        out_specs=pl.BlockSpec(memory_space=pltpu.HBM),
        scratch_shapes=[
            pltpu.VMEM((local, 3, 2, order, order), bf16),
            pltpu.VMEM((2, local, 2, order, order), bf16),
            pltpu.VMEM((order, order), bf16),
            pltpu.VMEM((2, local, 2, 2, order, order), bf16),
            pltpu.VMEM((local, 2 * order, 2 * order), jnp.float32),
            pltpu.VMEM(share, bf16),
            pltpu.VMEM(share, bf16),
            pltpu.VMEM(series, jnp.float32),
            pltpu.VMEM(lags, bf16),
            pltpu.VMEM(lags, bf16),
            pltpu.VMEM((2, local, 2, order, order), bf16),
            dma((2,)),
            dma((local, 2)),
            dma,
            dma((2, local)),
            dma((2, local)),
            dma,
            dma((2, peers)),
            dma,
            dma((2, 2)),
        ],
        compiler_params=pltpu.CompilerParams(
            collective_id=0, has_side_effects=True, vmem_limit_bytes=64 * 2**20 - 2**15
        ),
    )(green_lower, green_diag, green_upper, self_energy, coulomb)


def body(green_lower, green_diag, green_upper, self_energy, coulomb):
    peers = lax.axis_size("energy")
    blocks, order = green_diag.shape[0], green_diag.shape[-1]
    if blocks == 1 and order == 128 and order == peers * ROWS and peers & (peers - 1) == 0:
        return fused_body(green_lower, green_diag, green_upper, self_energy, coulomb)
    return plain_body(green_lower, green_diag, green_upper, self_energy, coulomb)


def solution(mesh):
    in_specs = (
        P("space", "energy", None, None, None),
        P("space", "energy", None, None, None),
        P("space", "energy", None, None, None),
        P(None, "space", "energy", None, None, None),
        P("space", None, None),
    )
    out_specs = P(None, "space", "energy", None, None, None)
    return jax.shard_map(body, mesh=mesh, in_specs=in_specs, out_specs=out_specs, check_vma=False)
```

profile of v0, /device:TPU:1, one launch (start us, length us, event | category | flops | bytes accessed | tf_op | source)
XLA Modules:
  0.0 37.5 jit_solution(2182260684031277651)
XLA Ops:
  0.0 35.6 %shard_map.55 = bf16[2,1,4,2,128,128]{5,4,3,2,1,0:T(8,128)(2,1)} custom-call(bf16[1,4,2,128,128]{4,3,2,1,0:T(8,128)(2,1)} %lower_hbm.1, bf16[1,4,2,128,128]{4,3,2,1,0:T(8,128)(2,1)} %diag_hbm.1, bf16[1,4,2,128,128]{4,3,2,1,0:T(8,128)(2,1)} %upper_hbm.1, bf16[2,1,4,2,128,128]{5,4,3,2,1,0:T(8,128)(2,1)} %sigma_hbm.1, bf16[1,128,128]{2,1,0:T(8,128)(2,1)} %coulomb_hbm.1), custom_call_target="tpu_custom_call" | custom-call | tf_op jit(solution)/shard_map/pallas_call | solution.py:508
  35.6 1.9 %copy.7 = bf16[2,1,4,2,128,128]{5,4,3,2,1,0:T(8,128)(2,1)} copy(bf16[2,1,4,2,128,128]{5,4,3,2,1,0:T(8,128)(2,1)} %shard_map.55) | data formatting | bytes 1048576
where the time goes:
time: 38 us; the launch traced here: 37.5 us
  Pallas kernels  35.6 us (94%)
  local copies, waits for them, and re-layouts  1.89 us (5%)
    pallas_call x1, Pallas kernels, fused_body(): pl.pallas_call(functools.partial(fused_kernel, peers, sites), out_shape=j...  35.6 us
    unnamed x1, local copies, waits for them, and re-layouts  1.89 us

commit v1 on v0

--- a/solution.py
+++ b/solution.py
@@ -178,7 +178,7 @@
     upper_hbm,
     sigma_hbm,
     coulomb_hbm,
-    out_hbm,
+    out_ref,
     greens,
     sigma_ref,
     coulomb_ref,
@@ -189,8 +189,6 @@
     series,
     polar_out,
     polar_in,
-    out_ref,
-    out_sem,
     load_sem,
     coulomb_sem,
     halo_send,
@@ -274,19 +272,23 @@
     def _():
         halo[1] = jnp.zeros(halo.shape[1:], halo.dtype)
 
-    def green_copy(side, other, slot, first, count):
+    early = max(local - 2, 0)
+
+    def green_copy(other, slot, group, energies_sent, sides_sent):
         return pltpu.make_async_remote_copy(
-            src_ref=green_out.at[side, other, pl.ds(first, count)],
-            dst_ref=green_in.at[side, slot, pl.ds(first, count)],
+            src_ref=green_out.at[other, energies_sent, sides_sent],
+            dst_ref=green_in.at[slot, energies_sent, sides_sent],
             send_sem=green_send,
-            recv_sem=green_recv.at[side, slot],
+            recv_sem=green_recv.at[group, slot],
             device_id={"energy": other},
             device_id_type=MESH,
         )
 
-    def send_green(side, first, count):
+    def send_green(group, first, count, side, sides):
         for step in steps:
-            green_copy(side, partner(me, step), me, first, count).start()
+            green_copy(
+                partner(me, step), me, group, pl.ds(first, count), pl.ds(side, sides)
+            ).start()
 
     def term(energy, terms):
         mixed, adjoint = [], []
@@ -352,11 +354,12 @@
                 block = rounded[
                     kind * order : (kind + 1) * order, side * order : (side + 1) * order
                 ]
-                green_out[side, :, energy, kind] = block.reshape(peers, ROWS, order)
-        first = energy - energy % 2
-        if energy % 2 == 1 or energy == local - 1:
+                green_out[:, energy, side, kind] = block.reshape(peers, ROWS, order)
+        if energy < early:
+            send_green(0, energy, 1, 0, 2)
+        elif energy == local - 1:
             for side in range(2):
-                send_green(side, first, energy + 1 - first)
+                send_green(side, early, local - early, side, 1)
         if energy + 2 < local:
             own_term(energy + 2)
 
@@ -398,12 +401,19 @@
             series[side, kind, 0, where] = jnp.where(low_lanes, top, swap(bottom))
             series[side, kind, 1, where] = jnp.where(low_lanes, swap(top), bottom)
 
+    def units_of(ref, slot, units):
+        if units % 2 == 0:
+            return ref.at[slot, pl.ds(0, units // 2)]
+        return ref.at[slot, pl.ds(0, units), 0]
+
     def receive_green(side):
-        unpack(side, me, green_out[side, me])
+        unpack(side, me, green_out[me, :, side])
         for step in steps:
             other = partner(me, step)
-            green_copy(side, other, other, 0, local).wait_recv()
-            unpack(side, other, green_in[side, other])
+            units = 2 * early * (1 - side) + local - early
+            arrived = units_of(green_in, other, units)
+            pltpu.make_async_copy(arrived, arrived, green_recv.at[side, other]).wait()
+            unpack(side, other, green_in[other, :, side])
 
     factor = 1.0 / math.sqrt(energies)
 
@@ -436,12 +446,13 @@
             tiles.append(jnp.concatenate([top, bottom], axis=1).astype(bf16))
         return tiles
 
-    def polar_copy(side, other, slot, kind):
+    def polar_copy(other, slot, kind):
+        where = (0,) if kind is None else (1, kind)
         return pltpu.make_async_remote_copy(
-            src_ref=polar_out.at[side, kind, other],
-            dst_ref=polar_in.at[side, kind, slot],
+            src_ref=polar_out.at[where[0], other, *where[1:]],
+            dst_ref=polar_in.at[where[0], slot, *where[1:]],
             send_sem=polar_send,
-            recv_sem=polar_recv.at[side, kind],
+            recv_sem=polar_recv.at[0 if kind is None else 1 + kind],
             device_id={"energy": other},
             device_id_type=MESH,
         )
@@ -452,27 +463,25 @@
             other = partner(me, step)
             tiles = correlate(side, other)
             for kind in range(2):
-                polar_out[side, kind, other] = tiles[kind]
-            for kind in range(2 if side == 0 else 1):
-                polar_copy(side, other, me, kind).start()
+                polar_out[side, other, kind] = tiles[kind]
+            polar_copy(other, me, None if side == 0 else 0).start()
         if side == 1:
             for step in steps:
-                polar_copy(side, partner(me, step), me, 1).start()
+                polar_copy(partner(me, step), me, 1).start()
         tiles = correlate(side, me)
         for kind in range(2):
-            polar_in[side, kind, me] = tiles[kind]
-
-    def out_copy(kind):
-        return pltpu.make_async_copy(out_ref.at[kind], out_hbm.at[kind, 0], out_sem.at[kind])
+            polar_in[side, me, kind] = tiles[kind]
 
     for kind in range(2):
-        for side in range(2):
-            arrived = polar_in.at[side, kind, pl.ds(0, peers - 1)]
-            pltpu.make_async_copy(arrived, arrived, polar_recv.at[side, kind]).wait()
+        if kind == 0:
+            arrived = polar_in.at[0, pl.ds(0, peers - 1)]
+            pltpu.make_async_copy(arrived, arrived, polar_recv.at[0]).wait()
+        arrived = polar_in.at[1, pl.ds(0, peers - 1), kind]
+        pltpu.make_async_copy(arrived, arrived, polar_recv.at[1 + kind]).wait()
         lefts = []
         for lag in range(local):
             both = jnp.concatenate(
-                [polar_in[side, kind, :, lag].reshape(order, order) for side in range(2)], axis=1
+                [polar_in[side, :, kind, lag].reshape(order, order) for side in range(2)], axis=1
             )
             lefts.append(jnp.dot(coulomb, both, preferred_element_type=f32).astype(bf16))
         screened = lax.dot_general(
@@ -483,33 +492,29 @@
         ).astype(bf16)
         for lag in range(local):
             rows = screened[lag * order : (lag + 1) * order]
-            out_ref[kind, lag, 0] = rows[:, :order]
-            out_ref[kind, lag, 1] = rows[:, order:]
-        out_copy(kind).start()
-
-    for sent, sem in ((green_out, green_send), (polar_out, polar_send)):
-        if sent is green_out:
-            part = sent.at[:, pl.ds(0, peers - 1)]
-        else:
-            part = sent.at[:, :, pl.ds(0, peers - 1)]
-        pltpu.make_async_copy(part, part, sem).wait()
-    for kind in range(2):
-        out_copy(kind).wait()
+            out_ref[kind, 0, lag, 0] = rows[:, :order]
+            out_ref[kind, 0, lag, 1] = rows[:, order:]
+
+    part = green_out.at[pl.ds(0, peers - 1)]
+    pltpu.make_async_copy(part, part, green_send).wait()
+    part = polar_out.at[:, pl.ds(0, peers - 1)]
+    pltpu.make_async_copy(part, part, polar_send).wait()
 
 
 def fused_body(green_lower, green_diag, green_upper, self_energy, coulomb):
     peers, sites = lax.axis_size("energy"), lax.axis_size("space")
     local, order = green_diag.shape[1], green_diag.shape[-1]
     bf16 = jnp.bfloat16
-    share = (2, peers, local, 2, ROWS, order)
-    lags = (2, 2, peers, local, ROWS, order)
+    share = (peers, local, 2, 2, ROWS, order)
+    lags = (2, peers, 2, local, ROWS, order)
     series = (2, 2, 2, peers * local + local, ROWS // 2, order)
     dma = pltpu.SemaphoreType.DMA
+    room = 64 * 2**20 - 2 * self_energy.size - 2**17
     return pl.pallas_call(
         functools.partial(fused_kernel, peers, sites),
-        out_shape=jax.ShapeDtypeStruct(self_energy.shape, bf16),
+        out_shape=pltpu.VMEM(self_energy.shape, bf16),
         in_specs=[pl.BlockSpec(memory_space=pltpu.HBM)] * 5,
-        out_specs=pl.BlockSpec(memory_space=pltpu.HBM),
+        out_specs=pl.BlockSpec(memory_space=pltpu.VMEM),
         scratch_shapes=[
             pltpu.VMEM((local, 3, 2, order, order), bf16),
             pltpu.VMEM((2, local, 2, order, order), bf16),
@@ -521,8 +526,6 @@
             pltpu.VMEM(series, jnp.float32),
             pltpu.VMEM(lags, bf16),
             pltpu.VMEM(lags, bf16),
-            pltpu.VMEM((2, local, 2, order, order), bf16),
-            dma((2,)),
             dma((local, 2)),
             dma,
             dma((2, local)),
@@ -530,10 +533,10 @@
             dma,
             dma((2, peers)),
             dma,
-            dma((2, 2)),
+            dma((3,)),
         ],
         compiler_params=pltpu.CompilerParams(
-            collective_id=0, has_side_effects=True, vmem_limit_bytes=64 * 2**20 - 2**15
+            collective_id=0, has_side_effects=True, vmem_limit_bytes=room
         ),
     )(green_lower, green_diag, green_upper, self_energy, coulomb)
 

time: 38 us -> 34.1 us (0.90)
  Pallas kernels: 35.6 us -> 33.2 us
  local copies, waits for them, and re-layouts: 1.89 us -> 0.8 us
    pallas_call x1, Pallas kernels: 35.6 us -> 33.2 us  [fused_body(): pl.pallas_call(functools.partial(fused_kernel, peers, sites), out_shape=p...]
    unnamed x1, local copies, waits for them, and re-layouts: 1.89 us -> 0.8 us
where the time goes in v1:
time: 34.1 us; the launch traced here: 34 us
  Pallas kernels  33.2 us (97%)
  local copies, waits for them, and re-layouts  0.8 us (2%)
    pallas_call x1, Pallas kernels, fused_body(): pl.pallas_call(functools.partial(fused_kernel, peers, sites), out_shape=p...  33.2 us
    unnamed x1, local copies, waits for them, and re-layouts  0.8 us

profile of v1, /device:TPU:1, one launch (start us, length us, event | category | flops | bytes accessed | tf_op | source)
XLA Modules:
  0.0 34.0 jit_solution(12279402340917604729)
XLA Ops:
  0.0 33.2 %shard_map.55 = bf16[2,1,4,2,128,128]{5,4,3,2,1,0:T(8,128)(2,1)S(1)} custom-call(bf16[1,4,2,128,128]{4,3,2,1,0:T(8,128)(2,1)} %lower_hbm.1, bf16[1,4,2,128,128]{4,3,2,1,0:T(8,128)(2,1)} %diag_hbm.1, bf16[1,4,2,128,128]{4,3,2,1,0:T(8,128)(2,1)} %upper_hbm.1, bf16[2,1,4,2,128,128]{5,4,3,2,1,0:T(8,128)(2,1)} %sigma_hbm.1, bf16[1,128,128]{2,1,0:T(8,128)(2,1)} %coulomb_hbm.1), custom_call_target="tpu_custom_call" | custom-call | tf_op jit(solution)/shard_map/pallas_call | solution.py:513
  33.2 0.8 %copy.7 = bf16[2,1,4,2,128,128]{5,4,3,2,1,0:T(8,128)(2,1)} copy(bf16[2,1,4,2,128,128]{5,4,3,2,1,0:T(8,128)(2,1)S(1)} %shard_map.55) | data formatting | bytes 1048576

commit v2 on v1

--- a/solution.py
+++ b/solution.py
@@ -183,7 +183,6 @@
     sigma_ref,
     coulomb_ref,
     halo,
-    total,
     green_out,
     green_in,
     series,
@@ -261,8 +260,7 @@
         def _():
             act(halo_copy(1, energy))
 
-    for energy in range(min(2, local)):
-        each_halo(energy, lambda copy: copy.start())
+    each_halo(0, lambda copy: copy.start())
 
     @pl.when(jnp.logical_not(has_previous))
     def _():
@@ -324,11 +322,12 @@
     def own_term(energy):
         load_sigma(energy).wait()
         pltpu.make_async_copy(greens.at[energy], greens.at[energy], load_sem.at[energy, 1]).wait()
-        total[energy] = term(energy, [(0, lambda kind, part: sigma_ref[kind, energy, part])])
-
-    for energy in range(min(2, local)):
-        own_term(energy)
+        return term(energy, [(0, lambda kind, part: sigma_ref[kind, energy, part])])
+
     for energy in range(local):
+        total = own_term(energy)
+        if energy + 1 < local:
+            each_halo(energy + 1, lambda copy: copy.start())
 
         @pl.when(has_previous)
         def _():
@@ -339,8 +338,6 @@
             halo_copy(1, energy).wait_recv()
 
         each_halo(energy, lambda copy: copy.wait_send())
-        if energy + 2 < local:
-            each_halo(energy + 2, lambda copy: copy.start())
         coupled = term(
             energy,
             [
@@ -348,7 +345,7 @@
                 (2, lambda kind, part: halo[1, energy, kind, part]),
             ],
         )
-        rounded = (total[energy] + coupled).astype(bf16)
+        rounded = (total + coupled).astype(bf16)
         for side in range(2):
             for kind in range(2):
                 block = rounded[
@@ -360,8 +357,6 @@
         elif energy == local - 1:
             for side in range(2):
                 send_green(side, early, local - early, side, 1)
-        if energy + 2 < local:
-            own_term(energy + 2)
 
     coulomb_load.wait()
     coulomb = coulomb_ref[...]
@@ -520,7 +515,6 @@
             pltpu.VMEM((2, local, 2, order, order), bf16),
             pltpu.VMEM((order, order), bf16),
             pltpu.VMEM((2, local, 2, 2, order, order), bf16),
-            pltpu.VMEM((local, 2 * order, 2 * order), jnp.float32),
             pltpu.VMEM(share, bf16),
             pltpu.VMEM(share, bf16),
             pltpu.VMEM(series, jnp.float32),

time: 34.1 us -> 35 us (1.026)
  Pallas kernels: 33.2 us -> 34 us
    pallas_call x1, Pallas kernels: 33.2 us -> 34 us  [fused_body(): pl.pallas_call(functools.partial(fused_kernel, peers, sites), out_shape=p...]
where the time goes in v2:
time: 35 us; the launch traced here: 34.8 us
  Pallas kernels  34 us (97%)
  local copies, waits for them, and re-layouts  0.8 us (2%)
    pallas_call x1, Pallas kernels, fused_body(): pl.pallas_call(functools.partial(fused_kernel, peers, sites), out_shape=p...  34 us
    unnamed x1, local copies, waits for them, and re-layouts  0.8 us

profile of v2, /device:TPU:1, one launch (start us, length us, event | category | flops | bytes accessed | tf_op | source)
XLA Modules:
  0.0 34.8 jit_solution(806701999490152933)
XLA Ops:
  0.0 34.0 %shard_map.55 = bf16[2,1,4,2,128,128]{5,4,3,2,1,0:T(8,128)(2,1)S(1)} custom-call(bf16[1,4,2,128,128]{4,3,2,1,0:T(8,128)(2,1)} %lower_hbm.1, bf16[1,4,2,128,128]{4,3,2,1,0:T(8,128)(2,1)} %diag_hbm.1, bf16[1,4,2,128,128]{4,3,2,1,0:T(8,128)(2,1)} %upper_hbm.1, bf16[2,1,4,2,128,128]{5,4,3,2,1,0:T(8,128)(2,1)} %sigma_hbm.1, bf16[1,128,128]{2,1,0:T(8,128)(2,1)} %coulomb_hbm.1), custom_call_target="tpu_custom_call" | custom-call | tf_op jit(solution)/shard_map/pallas_call | solution.py:508
  34.0 0.8 %copy.7 = bf16[2,1,4,2,128,128]{5,4,3,2,1,0:T(8,128)(2,1)} copy(bf16[2,1,4,2,128,128]{5,4,3,2,1,0:T(8,128)(2,1)S(1)} %shard_map.55) | data formatting | bytes 1048576

commit v3 on v1

--- a/solution.py
+++ b/solution.py
@@ -261,7 +261,7 @@
         def _():
             act(halo_copy(1, energy))
 
-    for energy in range(min(2, local)):
+    for energy in range(local):
         each_halo(energy, lambda copy: copy.start())
 
     @pl.when(jnp.logical_not(has_previous))
@@ -338,9 +338,6 @@
         def _():
             halo_copy(1, energy).wait_recv()
 
-        each_halo(energy, lambda copy: copy.wait_send())
-        if energy + 2 < local:
-            each_halo(energy + 2, lambda copy: copy.start())
         coupled = term(
             energy,
             [
@@ -357,9 +354,10 @@
                 green_out[:, energy, side, kind] = block.reshape(peers, ROWS, order)
         if energy < early:
             send_green(0, energy, 1, 0, 2)
-        elif energy == local - 1:
-            for side in range(2):
-                send_green(side, early, local - early, side, 1)
+        else:
+            send_green(0, energy, 1, 0, 1)
+        if energy == local - 1:
+            send_green(1, early, local - early, 1, 1)
         if energy + 2 < local:
             own_term(energy + 2)
 
@@ -495,6 +493,8 @@
             out_ref[kind, 0, lag, 0] = rows[:, :order]
             out_ref[kind, 0, lag, 1] = rows[:, order:]
 
+    for energy in range(local):
+        each_halo(energy, lambda copy: copy.wait_send())
     part = green_out.at[pl.ds(0, peers - 1)]
     pltpu.make_async_copy(part, part, green_send).wait()
     part = polar_out.at[:, pl.ds(0, peers - 1)]

time: 34.1 us -> 33.5 us (0.982)
  Pallas kernels: 33.2 us -> 32.6 us
    pallas_call x1, Pallas kernels: 33.2 us -> 32.6 us  [fused_body(): pl.pallas_call(functools.partial(fused_kernel, peers, sites), out_shape=p...]
where the time goes in v3:
time: 33.5 us; the launch traced here: 33.4 us
  Pallas kernels  32.6 us (97%)
  local copies, waits for them, and re-layouts  0.8 us (2%)
    pallas_call x1, Pallas kernels, fused_body(): pl.pallas_call(functools.partial(fused_kernel, peers, sites), out_shape=p...  32.6 us
    unnamed x1, local copies, waits for them, and re-layouts  0.8 us

profile of v3, /device:TPU:1, one launch (start us, length us, event | category | flops | bytes accessed | tf_op | source)
XLA Modules:
  0.0 33.4 jit_solution(8179606738723385518)
XLA Ops:
  0.0 32.6 %shard_map.55 = bf16[2,1,4,2,128,128]{5,4,3,2,1,0:T(8,128)(2,1)S(1)} custom-call(bf16[1,4,2,128,128]{4,3,2,1,0:T(8,128)(2,1)} %lower_hbm.1, bf16[1,4,2,128,128]{4,3,2,1,0:T(8,128)(2,1)} %diag_hbm.1, bf16[1,4,2,128,128]{4,3,2,1,0:T(8,128)(2,1)} %upper_hbm.1, bf16[2,1,4,2,128,128]{5,4,3,2,1,0:T(8,128)(2,1)} %sigma_hbm.1, bf16[1,128,128]{2,1,0:T(8,128)(2,1)} %coulomb_hbm.1), custom_call_target="tpu_custom_call" | custom-call | tf_op jit(solution)/shard_map/pallas_call | solution.py:513
  32.6 0.8 %copy.7 = bf16[2,1,4,2,128,128]{5,4,3,2,1,0:T(8,128)(2,1)} copy(bf16[2,1,4,2,128,128]{5,4,3,2,1,0:T(8,128)(2,1)S(1)} %shard_map.55) | data formatting | bytes 1048576

commit v4 on v3

--- a/solution.py
+++ b/solution.py
@@ -152,11 +152,11 @@
     return other
 
 
-def alternate(peers):
-    far, near = list(range(peers // 2, peers)), list(range(1, peers // 2))
-    steps = []
-    for i in range(peers // 2):
-        steps += far[i : i + 1] + near[i : i + 1]
+def far_first(peers):
+    steps, span = [], peers // 2
+    while span >= 1:
+        steps += list(range(span, 2 * span))
+        span //= 2
     return steps
 
 
@@ -207,7 +207,7 @@
     local, order = greens.shape[0], greens.shape[-1]
     half = order // 2
     energies = peers * local
-    steps = alternate(peers)
+    steps = far_first(peers)
     f32, bf16 = jnp.float32, jnp.bfloat16
 
     barrier = pltpu.get_barrier_semaphore()

time: 33.5 us -> 33.4 us (level)
  no operation moved by 1% of the time
where the time goes in v4:
time: 33.4 us; the launch traced here: 33.2 us
  Pallas kernels  32.4 us (97%)
  local copies, waits for them, and re-layouts  0.8 us (2%)
    pallas_call x1, Pallas kernels, fused_body(): pl.pallas_call(functools.partial(fused_kernel, peers, sites), out_shape=p...  32.4 us
    unnamed x1, local copies, waits for them, and re-layouts  0.8 us

profile of v4, /device:TPU:1, one launch (start us, length us, event | category | flops | bytes accessed | tf_op | source)
XLA Modules:
  0.0 33.2 jit_solution(10896675769841158436)
XLA Ops:
  0.0 32.4 %shard_map.55 = bf16[2,1,4,2,128,128]{5,4,3,2,1,0:T(8,128)(2,1)S(1)} custom-call(bf16[1,4,2,128,128]{4,3,2,1,0:T(8,128)(2,1)} %lower_hbm.1, bf16[1,4,2,128,128]{4,3,2,1,0:T(8,128)(2,1)} %diag_hbm.1, bf16[1,4,2,128,128]{4,3,2,1,0:T(8,128)(2,1)} %upper_hbm.1, bf16[2,1,4,2,128,128]{5,4,3,2,1,0:T(8,128)(2,1)} %sigma_hbm.1, bf16[1,128,128]{2,1,0:T(8,128)(2,1)} %coulomb_hbm.1), custom_call_target="tpu_custom_call" | custom-call | tf_op jit(solution)/shard_map/pallas_call | solution.py:513
  32.4 0.8 %copy.7 = bf16[2,1,4,2,128,128]{5,4,3,2,1,0:T(8,128)(2,1)} copy(bf16[2,1,4,2,128,128]{5,4,3,2,1,0:T(8,128)(2,1)S(1)} %shard_map.55) | data formatting | bytes 1048576
